TPU v7x, 256 devices: a whole 4x4x8 slice. The times are simulated.
256 devices in a mesh: seq: 32 (over x, y, core), tp: 8 (over z).
Axes of the slice: x: 4, y: 4, z: 8, core: 2. Of those that a mesh axis runs over, the one named last changes fastest.
Arguments:
- tokens: bfloat16 [65536, 16384], P('seq', 'tp'), may hold values from -120 to 120
- sketch: float32 [16384, 256], P('tp'), may hold values from -0.046875 to 0.046875
Outputs:
- basis: float32 [65536, 256], P('seq')
- coefficients: float32 [256, 16384], P('seq', 'tp')
All inputs are finite; a program needn't handle non-finite values.
Results may differ from a plain program's by a relative error of at most 0.0003.
Values sent between devices are 32-bit elements; how exact they have to be, the bound alone decides.
A program may use at most 64 MiB of HBM per device.

v0:
```python
import math

import jax
import jax.numpy as jnp
from jax import lax
from jax.sharding import PartitionSpec as P


def split_parts(matrix):
    high = matrix.astype(jnp.bfloat16)
    kept = lax.optimization_barrier(high)
    low = (matrix - kept.astype(matrix.dtype)).astype(jnp.bfloat16)
    return (high, low)


def shards(tokens, sketch):
    tok_rows = tokens.shape[0]
    seq_count = lax.axis_size("seq")
    total = tok_rows * seq_count
    columns_k = sketch.shape[1]
    sketch_high, sketch_low = split_parts(sketch)
    stacked = jnp.concatenate([sketch_high, sketch_low], axis=1)
    both = jnp.dot(tokens, stacked, preferred_element_type=jnp.float32)
    partial_value = both[:, :columns_k] + both[:, columns_k:]
    sketched = lax.psum(partial_value, "tp")
    local_gram = jnp.dot(
        sketched.T, sketched, precision=lax.Precision.HIGHEST, preferred_element_type=jnp.float32
    )
    gram = lax.psum(local_gram, "seq")
    lower = jnp.linalg.cholesky(gram)
    basis_t = jax.scipy.linalg.solve_triangular(lower, sketched.T, lower=True) * math.sqrt(total)
    basis_high, basis_low = split_parts(basis_t)
    term = jnp.dot(basis_high, tokens, preferred_element_type=jnp.float32)
    term = term + jnp.dot(basis_low, tokens, preferred_element_type=jnp.float32)
    coefficients = lax.psum_scatter(term / total, "seq", scatter_dimension=0, tiled=True)
    return (basis_t.T, coefficients)


def solution(mesh):
    return jax.shard_map(
        shards,
        mesh=mesh,
        in_specs=(P("seq", "tp"), P("tp", None)),
        out_specs=(P("seq", None), P("seq", "tp")),
        check_vma=False,
    )
```

profile of v0, /device:TPU:1, one launch (start us, length us, event | category | flops | bytes accessed | tf_op | source)
XLA Modules:
  0.0 385.6 jit_solution(5787527801276487807)
XLA Ops:
  7.2 1.8 convert_element_type.18
  9.7 7.0 %convolution_bitcast_fusion = f32[2048,512]{0,1:T(8,128)S(1)} fusion(bf16[2048,2048]{1,0:T(8,128)(2,1)} %param.2, bf16[2048,256]{1,0:T(8,128)(2,1)S(1)} %subtract_convert_fusion.1, bf16[2048,256]{1,0:T(8,128)(2,1)S(1)} %convert_element_type.18), kind=kOutput, calls=%fused_computation.2 | convolution fusion | flops 4299161600 | bytes 14680064 | tf_op jit(solution)/shard_map/dot_general | solution.py:23
  16.7 1.6 slice_add_fusion
  18.3 82.7 %all-reduce.4.cloned.1.call-done = f32[2048,256]{0,1:T(8,128)} async-done(((f32[2048,256]{0,1:T(8,128)}), f32[2048,256]{0,1:T(8,128)}) %all-reduce.4.cloned.1.call-update) | async-done | bytes 2097168 | tf_op jit(solution)/shard_map/psum | solution.py:25
  101.1 4.8 %fusion.19 = f32[256,256]{0,1:T(8,128)} fusion(f32[2048,256]{0,1:T(8,128)} %all-reduce.4.cloned.1.call-done), kind=kOutput, calls=%fused_computation.44 | convolution fusion | flops 1610612736 | bytes 2359296 | tf_op jit(solution)/shard_map/dot_general | solution.py:26
  106.1 113.1 %all-reduce.6.cloned.1.call-done = f32[256,256]{0,1:T(8,128)} async-done(((f32[256,256]{0,1:T(8,128)}), f32[256,256]{0,1:T(8,128)}) %all-reduce.6.cloned.1.call-update) | async-done | bytes 262160 | tf_op jit(solution)/shard_map/psum | solution.py:29
  219.3 1.1 copy.5
  220.3 1.0 fusion.9
  221.4 11.7 %cholesky.50 = f32[128,128]{1,0:T(8,128)S(1)} custom-call(f32[128,128]{1,0:T(8,128)S(1)} %cholesky.118), custom_call_target="Cholesky" | custom-call | tf_op jit(solution)/shard_map/jit(cholesky)/cholesky | solution.py:30
  233.1 9.8 %custom-call.15 = f32[1,128,128]{1,2,0:T(8,128)S(1)} custom-call(f32[1,128,128]{2,1,0:T(8,128)S(1)} %get-tuple-element.27), custom_call_target="InvertDiagBlocksLowerTriangular" | custom-call | tf_op jit(solution)/shard_map/jit(cholesky)/cholesky | solution.py:30
  243.4 11.7 %cholesky.105 = f32[128,128]{1,0:T(8,128)S(1)} custom-call(f32[128,128]{1,0:T(8,128)S(1)} %convolution_subtract_fusion.1), custom_call_target="Cholesky" | custom-call | tf_op jit(solution)/shard_map/jit(cholesky)/cholesky | solution.py:30
  255.2 0.7 compare_reduce_fusion
  257.2 4.1 %while.1 = (s32[]{:T(128)}, f32[256,256]{1,0:T(8,128)S(1)}, s32[2,2]{1,0:T(2,128)S(1)}, f32[2,128,128]{2,1,0:T(8,128)S(1)}, s32[]{:T(128)}) while((s32[]{:T(128)}, f32[256,256]{1,0:T(8,128)S(1)}, s32[2,2]{1,0:T(2,128)S(1)}, f32[2,128,128]{2,1,0:T(8,128)S(1)}, s32[]{:T(128)}) %tuple.29), condition=%wide.while_cond, body=%wide.while_body.sunk | while | flops 2 | bytes 131189 | solution.py:31
  258.0 1.4 bitcast_dynamic-update-slice_fusion.2
  259.4 0.6 fusion.32
  260.0 1.4 bitcast_dynamic-update-slice_fusion.2
  261.3 19.7 %custom-call.16 = f32[2,128,128]{1,2,0:T(8,128)S(1)} custom-call(f32[2,128,128]{2,1,0:T(8,128)S(1)} %get-tuple-element.9), custom_call_target="InvertDiagBlocksLowerTriangular" | custom-call | tf_op jit(solution)/shard_map/jit(_solve_triangular)/triangular_solve | solution.py:31
  281.0 1.1 fusion.6
  282.1 1.0 convolution_subtract_fusion
  283.1 1.1 fusion.11
  284.5 5.9 %fusion.20 = f32[256,2048]{1,0:T(8,128)S(1)} fusion(bf16[256,2048]{1,0:T(8,128)(2,1)S(1)} %get-tuple-element.22, bf16[2048,2048]{1,0:T(8,128)(2,1)} %param.2), kind=kOutput, calls=%fused_computation.45 | convolution fusion | flops 2147483648 | bytes 11534336 | tf_op jit(solution)/shard_map/dot_general | solution.py:33
  290.5 3.8 fusion
  294.3 1.8 copy.6
  296.1 83.0 %reduce-scatter.2.cloned.1.call-done = f32[8,2048]{1,0:T(8,128)} async-done(((f32[256,2048]{1,0:T(8,128)}), f32[8,2048]{1,0:T(8,128)}) %reduce-scatter.2.cloned.1.call-update) | async-done | bytes 65552 | tf_op jit(solution)/shard_map/reduce_scatter | solution.py:35
  (30 shorter events, 2.6 us)
Async XLA Ops:
  7.2 2.2 copy-start.1
  7.2 93.9 %all-reduce.4.cloned.1.call-start = ((), (), s32[]{:S(2)}) async-start(), calls=%async_computation.1 | async-start | bytes 4194304 | tf_op jit(solution)/shard_map/psum | solution.py:25
  18.3 201.0 %all-reduce.6.cloned.1.call-start = ((), (), s32[]{:S(2)}) async-start(), calls=%async_computation.2 | async-start | bytes 524288 | tf_op jit(solution)/shard_map/psum | solution.py:29
  105.9 175.1 %copy-start = (f32[2048,256]{0,1:T(8,128)S(1)}, f32[2048,256]{0,1:T(8,128)}, u32[]{:S(2)}) copy-start(f32[2048,256]{0,1:T(8,128)} %all-reduce.4.cloned.1.call-done) | copy-start | bytes 6291460
  105.9 273.2 %reduce-scatter.2.cloned.1.call-start = ((), (), s32[]{:S(2)}) async-start(), calls=%async_computation.3 | async-start | bytes 2162688 | tf_op jit(solution)/shard_map/reduce_scatter | solution.py:35
  284.2 6.3 %slice-start = ((s8[8388608]{0:T(1024)(128)(4,1)}), s8[4194304]{0:T(1024)(128)(4,1)S(1)}, s32[]{:S(2)}) async-start(s8[8388608]{0:T(1024)(128)(4,1)} %bitcast.44), calls=%async_computation.4 | async-start | bytes 8388608
  284.5 5.9 %slice-start.1 = ((s8[8388608]{0:T(1024)(128)(4,1)}), s8[4194304]{0:T(1024)(128)(4,1)S(1)}, s32[]{:S(2)}) async-start(s8[8388608]{0:T(1024)(128)(4,1)} %bitcast.44), calls=%async_computation.5 | async-start | bytes 8388608
Sparse Core Ops, SparseCore 0:
  18.4 82.6 all-reduce.3
  106.0 113.2 all-reduce.5
  294.4 84.6 reduce-scatter.1
where the time goes:
time: 386 us
  waiting for transfers between devices  279 us (72%)
  other arithmetic  58.6 us (15%)
  matrix products  25.1 us (7%)
  between operations  15.2 us (4%)
  local copies, waits for them, and re-layouts  7.23 us (2%)
    psum x1, waiting for transfers between devices, shards(): gram = lax.psum(local_gram, 'seq')  113 us
    reduce_scatter x1, waiting for transfers between devices, shards(): lax.psum_scatter(term / total, 'seq', scatter_dimension=0, tiled=True)  83 us
    psum x1, waiting for transfers between devices, shards(): sketched = lax.psum(partial_value, 'tp')  82.7 us
    another operation x6, other arithmetic, shards(): lower = jnp.linalg.cholesky(gram)  34 us
    another operation x3, other arithmetic, shards(): jax.scipy.linalg.solve_triangular(lower, sketched.T, lower=True)  19.7 us
  transfers between devices with their start and end apart: 3, of which 3 were waited for; matrix products, arithmetic and copies ran while one was open for 0% of the time, Pallas kernels for 0%

commit v1 on v0

v1 whole, which is shorter than its diff:
```python
import functools
import math

import jax
import jax.numpy as jnp
from jax import lax
from jax.experimental import pallas as pl
from jax.experimental.pallas import tpu as pltpu
from jax.sharding import PartitionSpec as P

MESH = pl.DeviceIdType.MESH
HIGHEST = lax.Precision.HIGHEST
F32 = jnp.float32
BF16 = jnp.bfloat16
HALF = 128
PANEL = 8


def dot32(a, b, dims):
    return lax.dot_general(a, b, (dims, ((), ())), precision=HIGHEST, preferred_element_type=F32)


def nn(a, b):
    return dot32(a, b, ((1,), (0,)))


def nt(a, b):
    return dot32(a, b, ((1,), (1,)))


def tn(a, b):
    return dot32(a, b, ((0,), (0,)))


def split_parts(value):
    high = value.astype(BF16)
    low = (value - high.astype(F32)).astype(BF16)
    return high, low


def inverse_factor(matrix):
    size = matrix.shape[0]
    sub = lax.broadcasted_iota(jnp.int32, (PANEL, HALF), 0)
    lane = lax.broadcasted_iota(jnp.int32, (PANEL, HALF), 1)
    rest = matrix
    done = []
    for first in range(0, size, PANEL):
        panel = rest[:PANEL]
        below = rest[PANEL:]
        columns = [
            jnp.broadcast_to(panel[:, first + j : first + j + 1], (PANEL, HALF)) for j in range(PANEL)
        ]
        inside = (lane >= first) & (lane < first + PANEL)
        panel = jnp.where(inside, jnp.where(lane - first == sub, 1.0, 0.0), panel)
        work = columns + [panel]
        kept = jnp.zeros((PANEL, HALF), F32)
        pivots = jnp.ones((PANEL, HALF), F32)
        for j in range(PANEL):
            here = sub == j
            rows = [jnp.broadcast_to(item[j : j + 1], (PANEL, HALF)) for item in work]
            pivot = rows[0]
            factor = jnp.where(here, -1.0, work[0]) * (1.0 / pivot)
            kept = jnp.where(here, rows[-1], kept)
            pivots = jnp.where(here, pivot, pivots)
            work = [
                jnp.where(here, 0.0, item) - factor * row for item, row in zip(work[1:], rows[1:])
            ]
        scaled = kept * lax.rsqrt(pivots)
        done.append(jnp.where(lane <= sub + first, scaled, 0.0))
        if first + PANEL < size:
            solved = work[0]
            count = size - first - PANEL
            below_lane = lax.broadcasted_iota(jnp.int32, (count, HALF), 1)
            update = jnp.where((below_lane >= first) & (below_lane < first + PANEL), 0.0, below)
            for j in range(PANEL):
                update = update - below[:, first + j : first + j + 1] * solved[j : j + 1]
            rest = update
        yield None
    return jnp.concatenate(done, axis=0)


def kernel(
    nq, nz, total,
    tok_hbm, sk_hbm, basis_out, coef_out,
    tok, sk, weights, part, ring, s_all,
    gsrc0, gsrc1, ga0, ga1, gb0, gb1, gfull0, gfull1,
    c0, cx, cp, cr, cg, outs, landed, basis_v,
    tok_sem, sk_sem, rs_send, rs_recv, ag_send, ag_recv, g_send, g_recv,
    c_send, c_recv, out_sem,
):
    rows, feats = tok.shape
    chunk = rows // nz
    unit = chunk // 2
    dist = nz // 2
    me = lax.axis_index("seq")
    z = lax.axis_index("tp")
    q, core = me // 2, lax.rem(me, 2)
    other = q * 2 + (1 - core)
    up, down = lax.rem(z + 1, nz), lax.rem(z + nz - 1, nz)
    members = 2 * nz
    mine = z * 2 + core

    def remote(src, dst, send, recv, seq_id, z_id):
        return pltpu.make_async_remote_copy(
            src_ref=src, dst_ref=dst, send_sem=send, recv_sem=recv,
            device_id=(seq_id, z_id), device_id_type=MESH,
        )

    def xy_peer(o):
        peer = lax.rem(q + o, nq)
        return peer, peer * 2 + core

    def zc_peer(o):
        peer = lax.rem(mine + o, members)
        return q * 2 + lax.rem(peer, 2), peer // 2

    def chunk_of(j):
        return lax.rem(z + j, nz)

    sk_copies = [
        pltpu.make_async_copy(sk_hbm.at[:, pl.ds(h * HALF, HALF)], sk.at[h], sk_sem.at[h])
        for h in range(2)
    ]
    tok_copies = {}
    order = [dist]
    for s in range(1, dist):
        order += [dist - s, nz - dist + s]
    order.append(0)
    for j in order:
        at = pl.ds(pl.multiple_of(chunk_of(j) * chunk, chunk), chunk)
        tok_copies[j] = pltpu.make_async_copy(tok_hbm.at[at], tok.at[at], tok_sem.at[j])
    sk_copies[0].start()
    tok_copies[order[0]].start()
    sk_copies[1].start()
    for j in order[1:]:
        tok_copies[j].start()

    barrier = pltpu.get_barrier_semaphore()

    def greet_xy(o, carry):
        _, seq_id = xy_peer(o)
        pl.semaphore_signal(barrier, inc=1, device_id=(seq_id, z), device_id_type=MESH)
        return carry

    def greet_zc(o, carry):
        seq_id, z_id = zc_peer(o)
        pl.semaphore_signal(barrier, inc=1, device_id=(seq_id, z_id), device_id_type=MESH)
        return carry

    lax.fori_loop(1, nq, greet_xy, 0)
    lax.fori_loop(1, members, greet_zc, 0)

    loaded = set()

    def prepare_weights(h):
        sk_copies[h].wait()
        step = min(256, feats)

        @pl.loop(0, feats // step)
        def _(i):
            at = pl.ds(pl.multiple_of(i * step, step), step)
            high, low = split_parts(sk[h, at, :])
            weights[h, at, :HALF] = high
            weights[h, at, HALF:] = low

    def compute_part(h, j):
        if j not in loaded:
            tok_copies[j].wait()
            loaded.add(j)
        at = pl.ds(pl.multiple_of(chunk_of(j) * chunk, chunk), chunk)
        both = jnp.dot(tok[at, :], weights[h], preferred_element_type=F32)
        part[h, j] = both[:, :HALF] + both[:, HALF:]

    def unit_rows(u):
        return pl.ds(u * unit, unit)

    sent = []

    def rs_copy(h, d, s, u, src):
        slot = s * 2 + u
        return remote(
            src, ring.at[h, d, slot], rs_send.at[h, d, slot], rs_recv.at[h, d, slot],
            me, up if d == 0 else down,
        )

    def rs_send_unit(h, d, s, u, src):
        copy = rs_copy(h, d, s, u, src)
        copy.start()
        sent.append(copy)

    def rs_wait(h, d, s, u):
        rs_copy(h, d, s, u, ring.at[h, d, s * 2 + u]).wait_recv()

    def reduce_scatter(h):
        prepare_weights(h)
        compute_part(h, dist)
        if h == 0:
            pl.semaphore_wait(barrier, nq - 1 + members - 1)
        for d in range(2):
            rs_send_unit(h, d, 0, d, part.at[h, dist, unit_rows(d)])
        yield
        for s in range(1, dist):
            places = (dist - s, nz - dist + s)
            for j in places:
                compute_part(h, j)
            if s == 1:
                for d in range(2):
                    u = 1 - d
                    rs_send_unit(h, d, 1, u, part.at[h, places[d], unit_rows(u)])
            yield
            for u_step in ([1] if s == 1 else [0, 1]):
                for d in range(2):
                    u = (1 - d) if u_step == 0 else d
                    rs_wait(h, d, s - 1, u)
                    slot = (s - 1) * 2 + u
                    ring[h, d, slot] = ring[h, d, slot] + part[h, places[d], unit_rows(u), :]
                    rs_send_unit(h, d, s, u, ring.at[h, d, slot])
            yield
        compute_part(h, 0)
        yield
        for u in range(2):
            for d in range(2):
                rs_wait(h, d, dist - 1, u) if (dist > 1 or u == d) else None
        at = pl.multiple_of(z * chunk, chunk)
        for u in range(2):
            slot = (dist - 1) * 2 + u
            value = part[h, 0, unit_rows(u), :] + ring[h, 0, slot] + ring[h, 1, slot]
            s_all[h, pl.ds(at + u * unit, unit), :] = value
        yield

    def ag_copy(h, d, k, u):
        c = lax.rem(z + nz - k, nz) if d == 0 else lax.rem(z + k, nz)
        at = pl.ds(pl.multiple_of(c * chunk + u * unit, unit), unit)
        slot = k * 2 + u
        return remote(
            s_all.at[h, at], s_all.at[h, at], ag_send.at[h, d, slot], ag_recv.at[h, d, slot],
            me, up if d == 0 else down,
        )

    def ag_arrived(h, d, k, u):
        c = lax.rem(z + nz - k - 1, nz) if d == 0 else lax.rem(z + k + 1, nz)
        at = pl.ds(pl.multiple_of(c * chunk + u * unit, unit), unit)
        slot = k * 2 + u
        remote(
            s_all.at[h, at], s_all.at[h, at], ag_send.at[h, d, slot], ag_recv.at[h, d, slot],
            me, up if d == 0 else down,
        ).wait_recv()

    def all_gather(h):
        for k in range(dist):
            for step in range(2):
                for d in range(2):
                    u = d if step == 0 else 1 - d
                    if k > 0:
                        ag_arrived(h, d, k - 1, u)
                    if k < dist - 1 or step == 0:
                        copy = ag_copy(h, d, k, u)
                        copy.start()
                        sent.append(copy)
            yield
        for d in range(2):
            ag_arrived(h, d, dist - 1, d)
        yield

    def spread(g, step, count, start_one, sized):
        def body(o, carry):
            start_one(o).start()
            return carry

        lax.fori_loop(1, count, body, 0)

        def wait_all():
            probe = remote(sized, sized, g_send.at[g, step], g_recv.at[g, step], me, up)
            probe.wait_recv()
            probe.wait_send()

        return wait_all

    def gram_sum(g, src, ga, gb, full):
        piece = src.shape[0] // nq

        def rows_of(i):
            return pl.ds(pl.multiple_of(i * piece, piece), piece)

        def first(o):
            peer, seq_id = xy_peer(o)
            return remote(
                src.at[rows_of(peer)], ga.at[q], g_send.at[g, 0], g_recv.at[g, 0], seq_id, z
            )

        wait_first = spread(g, 0, nq, first, ga.at[pl.ds(0, nq - 1)])
        ga[q] = src[rows_of(q), :]
        yield
        wait_first()
        value = ga[0]
        for i in range(1, nq):
            value = value + ga[i]
        gb[mine] = value

        def second(o):
            seq_id, z_id = zc_peer(o)
            return remote(gb.at[mine], gb.at[mine], g_send.at[g, 1], g_recv.at[g, 1], seq_id, z_id)

        wait_second = spread(g, 1, members, second, gb.at[pl.ds(0, members - 1)])
        yield
        wait_second()
        value = gb[0]
        for i in range(1, members):
            value = value + gb[i]
        full[rows_of(q), :] = value

        def third(o):
            _, seq_id = xy_peer(o)
            return remote(
                full.at[rows_of(q)], full.at[rows_of(q)], g_send.at[g, 2], g_recv.at[g, 2],
                seq_id, z,
            )

        wait_third = spread(g, 2, nq, third, full.at[pl.ds(0, (nq - 1) * piece)])
        yield
        wait_third()
        yield

    tile = min(512, feats)
    per_tile = tile // HALF

    def product(h, j, first, after_tile=None):
        at = pl.ds(pl.multiple_of(chunk_of(j) * chunk, chunk), chunk)
        high, low = split_parts(s_all[h, at, :].T)
        left = jnp.concatenate([high, low], axis=0)
        for t in range(feats // tile):
            both = jnp.dot(left, tok[at, t * tile : (t + 1) * tile], preferred_element_type=F32)
            value = both[:HALF] + both[HALF:]
            for i in range(per_tile):
                item = value[:, i * HALF : (i + 1) * HALF]
                p = t * per_tile + i
                c0[h, p] = item if first else c0[h, p] + item
            if after_tile is not None:
                after_tile(t)

    split = HALF // 2

    def core_copy(h, t):
        give = pl.ds(pl.multiple_of((1 - core) * split, split), split)
        at = pl.ds(t * per_tile, per_tile)
        return remote(
            c0.at[h, at, give], cx.at[h, at], c_send.at[h, t], c_recv.at[h, t], other, z
        )

    tiles = feats // tile

    def start_core(h):
        def after(t):
            copy = core_copy(h, t)
            copy.start()
            sent.append(copy)

        return after

    def coef_sum(h):
        keep = pl.ds(pl.multiple_of(core * split, split), split)
        for t in range(tiles):
            core_copy(h, t).wait_recv()
            for i in range(per_tile):
                p = t * per_tile + i
                cp[h, p] = c0[h, p, keep, :] + cx[h, p]

        def body(o, carry):
            peer, seq_id = xy_peer(o)
            remote(
                cp.at[h, peer], cr.at[h, q], c_send.at[h, tiles], c_recv.at[h, tiles], seq_id, z
            ).start()
            return carry

        lax.fori_loop(1, nq, body, 0)
        cr[h, q] = cp[h, q]
        yield
        sized = cr.at[h, pl.ds(0, nq - 1)]
        probe = remote(sized, sized, c_send.at[h, tiles], c_recv.at[h, tiles], me, up)
        probe.wait_recv()
        probe.wait_send()
        value = cr[h, 0]
        for i in range(1, nq):
            value = value + cr[h, i]
        cg[h, keep, :] = value
        copy = remote(
            cg.at[h, keep], cg.at[h, keep], c_send.at[h, tiles + 1], c_recv.at[h, tiles + 1],
            other, z,
        )
        copy.start()
        yield
        copy.wait()
        yield

    def run(gen, steps=None):
        count = 0
        while steps is None or count < steps:
            try:
                next(gen)
            except StopIteration as stop:
                return stop.value
            count += 1
        return None

    rs = [reduce_scatter(h) for h in range(2)]
    ag = [all_gather(h) for h in range(2)]
    coef = [coef_sum(h) for h in range(2)]
    rs_steps = 1 + 2 * (dist - 1)

    run(rs[0], rs_steps + 1)
    run(rs[1], 2)
    run(rs[0], 1)
    own = pl.ds(pl.multiple_of(z * chunk, chunk), chunk)
    own0 = s_all[0, own, :]
    gsrc0[...] = tn(own0, own0)
    gram0 = gram_sum(0, gsrc0, ga0, gb0, gfull0)
    run(gram0, 1)
    run(rs[1], 1)
    run(gram0, 1)
    run(rs[1], rs_steps - 3)
    run(ag[0], 1)
    run(gram0, 1)
    run(rs[1], 1)
    run(rs[1], 1)
    own1 = s_all[1, own, :]
    gsrc1[:HALF] = tn(own1, s_all[0, own, :])
    gsrc1[HALF:] = tn(own1, own1)
    gram1 = gram_sum(1, gsrc1, ga1, gb1, gfull1)
    run(gram1, 1)
    run(gram0, 1)
    chol0 = inverse_factor(gfull0[...])
    run(chol0, 3)
    run(gram1, 1)
    run(ag[0], 1)
    run(chol0, 4)
    run(gram1, 1)
    run(chol0, 3)
    run(ag[0], 1)
    w00 = run(chol0)
    run(gram1)
    low10 = nt(gfull1[:HALF], w00)
    run(ag[0], dist - 3 if dist > 3 else 0)
    run(ag[1], 1)
    schur = gfull1[HALF:] - nt(low10, low10)
    chol1 = inverse_factor(schur)
    run(chol1, 4)
    run(ag[0])
    run(chol1, 2)
    for i, j in enumerate(order):
        product(0, j, i == 0, start_core(0) if i == nz - 1 else None)
    run(ag[1], 1)
    run(chol1, 4)
    run(coef[0], 1)
    run(ag[1], 1)
    mixed = nn(low10, w00)
    w11 = run(chol1)
    run(ag[1], 1)
    w10 = -nn(w11, mixed)
    run(coef[0], 1)
    late = [dist]
    if dist > 1:
        late = [dist - 1, nz - dist + 1, dist]
    early = [j for j in order if j not in late]
    for i, j in enumerate(early):
        product(1, j, i == 0)
    run(ag[1])
    run(coef[0])
    for i, j in enumerate(late):
        last = i == len(late) - 1
        product(1, j, not early and i == 0, start_core(1) if last else None)
    run(coef[1], 1)

    root = math.sqrt(total)
    b00, b10, b11 = w00 * root, w10 * root, w11 * root
    basis_copies = []
    step = min(256, rows)
    for i in range(rows // step):
        at = pl.ds(i * step, step)
        left0, left1 = s_all[0, at, :], s_all[1, at, :]
        basis_v[at, :HALF] = nt(left0, b00)
        basis_v[at, HALF:] = nt(left0, b10) + nt(left1, b11)
        copy = pltpu.make_async_copy(basis_v.at[at], basis_out.at[at], out_sem.at[i])
        copy.start()
        basis_copies.append(copy)

    run(coef[1])
    block = 2 * HALF // (2 * nq)
    outs[:HALF] = nn(w00, cg[0]) / root
    outs[HALF:] = (nn(w10, cg[0]) + nn(w11, cg[1])) / root

    def rows_for(seq_id):
        return pl.ds(pl.multiple_of(seq_id * block, block), block)

    def last_hop(o, carry):
        _, seq_id = xy_peer(o)
        remote(
            outs.at[rows_for(seq_id)], landed.at[q], c_send.at[2, 0], c_recv.at[2, 0], seq_id, z
        ).start()
        return carry

    lax.fori_loop(1, nq, last_hop, 0)
    landed[q] = outs[rows_for(me), :]
    sized = landed.at[pl.ds(0, nq - 1)]
    probe = remote(sized, sized, c_send.at[2, 0], c_recv.at[2, 0], me, up)
    probe.wait_recv()
    probe.wait_send()
    for i in range(nq):
        coef_out[:, i * HALF : (i + 1) * HALF] = landed[i]

    for copy in sent:
        copy.wait_send()
    for copy in basis_copies:
        copy.wait()


def shards(mesh_shape, tokens, sketch):
    rows, feats = tokens.shape
    seq, nz = mesh_shape["seq"], mesh_shape["tp"]
    nq = seq // 2
    total = rows * seq
    chunk = rows // nz
    unit = chunk // 2
    dist = nz // 2
    k = 2 * HALF
    dma = pltpu.SemaphoreType.DMA
    tiles = feats // min(512, feats)
    return pl.pallas_call(
        functools.partial(kernel, nq, nz, total),
        out_shape=(
            jax.ShapeDtypeStruct((rows, k), F32),
            jax.ShapeDtypeStruct((k // seq, feats), F32),
        ),
        in_specs=[pl.BlockSpec(memory_space=pl.ANY)] * 2,
        out_specs=(pl.BlockSpec(memory_space=pl.ANY), pl.BlockSpec(memory_space=pltpu.VMEM)),
        scratch_shapes=[
            pltpu.VMEM((rows, feats), BF16),
            pltpu.VMEM((2, feats, HALF), F32),
            pltpu.VMEM((2, feats, k), BF16),
            pltpu.VMEM((2, nz, chunk, HALF), F32),
            pltpu.VMEM((2, 2, nz, unit, HALF), F32),
            pltpu.VMEM((2, rows, HALF), F32),
            pltpu.VMEM((HALF, HALF), F32),
            pltpu.VMEM((k, HALF), F32),
            pltpu.VMEM((nq, HALF // nq, HALF), F32),
            pltpu.VMEM((nq, k // nq, HALF), F32),
            pltpu.VMEM((2 * nz, HALF // nq, HALF), F32),
            pltpu.VMEM((2 * nz, k // nq, HALF), F32),
            pltpu.VMEM((HALF, HALF), F32),
            pltpu.VMEM((k, HALF), F32),
            pltpu.VMEM((2, nq, HALF, HALF), F32),
            pltpu.VMEM((2, nq, HALF // 2, HALF), F32),
            pltpu.VMEM((2, nq, HALF // 2, HALF), F32),
            pltpu.VMEM((2, nq, HALF // 2, HALF), F32),
            pltpu.VMEM((2, HALF, HALF), F32),
            pltpu.VMEM((k, HALF), F32),
            pltpu.VMEM((nq, k // seq, HALF), F32),
            pltpu.VMEM((rows, k), F32),
            dma((nz,)),
            dma((2,)),
            dma((2, 2, nz)),
            dma((2, 2, nz)),
            dma((2, 2, nz)),
            dma((2, 2, nz)),
            dma((2, 3)),
            dma((2, 3)),
            dma((3, tiles + 2)),
            dma((3, tiles + 2)),
            dma((max(1, rows // 256),)),
        ],
        compiler_params=pltpu.CompilerParams(
            collective_id=0, has_side_effects=True, vmem_limit_bytes=50 * 1024 * 1024
        ),
    )(tokens, sketch)


def solution(mesh):
    return jax.shard_map(
        functools.partial(shards, dict(mesh.shape)),
        mesh=mesh,
        in_specs=(P("seq", "tp"), P("tp", None)),
        out_specs=(P("seq", None), P("seq", "tp")),
        check_vma=False,
    )
```

time: 386 us -> 102 us (0.26)
  waiting for transfers between devices: 279 us -> 0 us
  Pallas kernels: 0 us -> 99 us
  other arithmetic: 58.6 us -> 0 us
  matrix products: 25.1 us -> 0 us
  between operations: 15.2 us -> 0.64 us
  local copies, waits for them, and re-layouts: 7.23 us -> 1.95 us
    psum x2 -> x0, waiting for transfers between devices: 196 us -> none  [the longest x1 113 us: shards(): gram = lax.psum(local_gram, 'seq')]
    pallas_call x0 -> x1, Pallas kernels: none -> 99 us  [shards(): pl.pallas_call(functools.partial(kernel, nq, nz, total), out_shape=(jax.S...]
    reduce_scatter x1 -> x0, waiting for transfers between devices: 83 us -> none  [shards(): lax.psum_scatter(term / total, 'seq', scatter_dimension=0, tiled=True)]
    another operation x9 -> x0, other arithmetic: 53.7 us -> none  [the longest x6 34 us: shards(): lower = jnp.linalg.cholesky(gram)]
    dot_general x4 -> x0, matrix products: 21.5 us -> none  [the longest x1 7.03 us: shards(): both = jnp.dot(tokens, stacked, preferred_element_type=jnp.float32)]
    another operation x9 -> x0, local copies, waits for them, and re-layouts: 3.99 us -> none
  transfers between devices with their start and end apart: 3 -> 0, of which waited for: 3 -> 0; matrix products, arithmetic and copies ran while one was open for 0% -> 0% of each run, Pallas kernels for 0% -> 0%
where the time goes in v1:
time: 102 us
  Pallas kernels  99 us (97%)
  local copies, waits for them, and re-layouts  1.95 us (2%)
    pallas_call x1, Pallas kernels, shards(): pl.pallas_call(functools.partial(kernel, nq, nz, total), out_shape=(jax.S...  99 us

profile of v1, /device:TPU:1, one launch (start us, length us, event | category | flops | bytes accessed | tf_op | source)
XLA Modules:
  0.0 101.6 jit_solution(8446582836326997549)
XLA Ops:
  0.6 99.0 %shard_map.41 = (f32[2048,256]{1,0:T(8,128)S(1)}, f32[8,2048]{1,0:T(8,128)S(1)}) custom-call(bf16[2048,2048]{1,0:T(8,128)(2,1)} %tok_hbm.1, f32[2048,256]{1,0:T(8,128)} %sk_hbm.1), custom_call_target="tpu_custom_call" | custom-call | tf_op jit(solution)/shard_map/pallas_call | solution.py:527
  99.6 1.3 %copy.6 = f32[2048,256]{1,0:T(8,128)} copy(f32[2048,256]{1,0:T(8,128)S(1)} %get-tuple-element.4) | data formatting | bytes 4194304
  100.9 0.6 copy.7

commit v2 on v1

--- a/solution.py
+++ b/solution.py
@@ -83,10 +83,10 @@
     nq, nz, total,
     tok_hbm, sk_hbm, basis_out, coef_out,
     tok, sk, weights, part, ring, s_all,
-    gsrc0, gsrc1, ga0, ga1, gb0, gb1, gfull0, gfull1,
-    c0, cx, cp, cr, cg, outs, landed, basis_v,
+    gsrc, ga, gb, gfull,
+    c0, cx, cp, cr, cg, outs, landed,
     tok_sem, sk_sem, rs_send, rs_recv, ag_send, ag_recv, g_send, g_recv,
-    c_send, c_recv, out_sem,
+    c_send, c_recv,
 ):
     rows, feats = tok.shape
     chunk = rows // nz
@@ -97,8 +97,7 @@
     q, core = me // 2, lax.rem(me, 2)
     other = q * 2 + (1 - core)
     up, down = lax.rem(z + 1, nz), lax.rem(z + nz - 1, nz)
-    members = 2 * nz
-    mine = z * 2 + core
+    seq_count = nq * 2
 
     def remote(src, dst, send, recv, seq_id, z_id):
         return pltpu.make_async_remote_copy(
@@ -110,9 +109,8 @@
         peer = lax.rem(q + o, nq)
         return peer, peer * 2 + core
 
-    def zc_peer(o):
-        peer = lax.rem(mine + o, members)
-        return q * 2 + lax.rem(peer, 2), peer // 2
+    def seq_peer(o):
+        return lax.rem(me + o, seq_count)
 
     def chunk_of(j):
         return lax.rem(z + j, nz)
@@ -137,18 +135,18 @@
 
     barrier = pltpu.get_barrier_semaphore()
 
-    def greet_xy(o, carry):
-        _, seq_id = xy_peer(o)
-        pl.semaphore_signal(barrier, inc=1, device_id=(seq_id, z), device_id_type=MESH)
+    def greet_seq(o, carry):
+        pl.semaphore_signal(barrier, inc=1, device_id=(seq_peer(o), z), device_id_type=MESH)
         return carry
 
-    def greet_zc(o, carry):
-        seq_id, z_id = zc_peer(o)
-        pl.semaphore_signal(barrier, inc=1, device_id=(seq_id, z_id), device_id_type=MESH)
+    def greet_z(o, carry):
+        pl.semaphore_signal(
+            barrier, inc=1, device_id=(me, lax.rem(z + o, nz)), device_id_type=MESH
+        )
         return carry
 
-    lax.fori_loop(1, nq, greet_xy, 0)
-    lax.fori_loop(1, members, greet_zc, 0)
+    lax.fori_loop(1, nz, greet_z, 0)
+    lax.fori_loop(1, seq_count, greet_seq, 0)
 
     loaded = set()
 
@@ -191,42 +189,15 @@
     def rs_wait(h, d, s, u):
         rs_copy(h, d, s, u, ring.at[h, d, s * 2 + u]).wait_recv()
 
-    def reduce_scatter(h):
-        prepare_weights(h)
-        compute_part(h, dist)
-        if h == 0:
-            pl.semaphore_wait(barrier, nq - 1 + members - 1)
-        for d in range(2):
-            rs_send_unit(h, d, 0, d, part.at[h, dist, unit_rows(d)])
-        yield
-        for s in range(1, dist):
-            places = (dist - s, nz - dist + s)
-            for j in places:
-                compute_part(h, j)
-            if s == 1:
-                for d in range(2):
-                    u = 1 - d
-                    rs_send_unit(h, d, 1, u, part.at[h, places[d], unit_rows(u)])
-            yield
-            for u_step in ([1] if s == 1 else [0, 1]):
-                for d in range(2):
-                    u = (1 - d) if u_step == 0 else d
-                    rs_wait(h, d, s - 1, u)
-                    slot = (s - 1) * 2 + u
-                    ring[h, d, slot] = ring[h, d, slot] + part[h, places[d], unit_rows(u), :]
-                    rs_send_unit(h, d, s, u, ring.at[h, d, slot])
-            yield
-        compute_part(h, 0)
-        yield
+    def own_chunk(h):
+        at = pl.multiple_of(z * chunk, chunk)
         for u in range(2):
             for d in range(2):
-                rs_wait(h, d, dist - 1, u) if (dist > 1 or u == d) else None
-        at = pl.multiple_of(z * chunk, chunk)
+                rs_wait(h, d, dist - 1, u)
         for u in range(2):
             slot = (dist - 1) * 2 + u
             value = part[h, 0, unit_rows(u), :] + ring[h, 0, slot] + ring[h, 1, slot]
             s_all[h, pl.ds(at + u * unit, unit), :] = value
-        yield
 
     def ag_copy(h, d, k, u):
         c = lax.rem(z + nz - k, nz) if d == 0 else lax.rem(z + k, nz)
@@ -246,79 +217,128 @@
             me, up if d == 0 else down,
         ).wait_recv()
 
-    def all_gather(h):
-        for k in range(dist):
-            for step in range(2):
-                for d in range(2):
-                    u = d if step == 0 else 1 - d
-                    if k > 0:
-                        ag_arrived(h, d, k - 1, u)
-                    if k < dist - 1 or step == 0:
-                        copy = ag_copy(h, d, k, u)
-                        copy.start()
-                        sent.append(copy)
-            yield
+    if dist == 4:
+        turns = [
+            (0, 0, 1, 0), (0, 0, 0, 1), (0, 1, 1, 0), (0, 0, 1, 1), (0, 0, 0, 2), (0, 1, 1, 1),
+            (0, 0, 1, 2), (0, 0, 0, 3), (0, 1, 0, 1), (0, 0, 1, 3), (0, 1, 1, 2), (0, 1, 0, 2),
+            (1, 0, 1, 0), (0, 1, 1, 3), (0, 1, 0, 3), (1, 0, 0, 0), (1, 0, 1, 1), (1, 1, 1, 0),
+            (1, 0, 0, 1), (1, 0, 1, 2), (1, 1, 0, 0), (1, 0, 0, 2), (1, 0, 1, 3), (1, 1, 1, 1),
+            (1, 1, 0, 1), (1, 1, 1, 2), (1, 1, 0, 2), (1, 1, 1, 3),
+        ]
+    else:
+        turns = [(0, h, x, k) for k in range(dist) for h in range(2) for x in (1, 0) if k or x]
+        turns += [
+            (1, h, x, k) for k in range(dist) for h in range(2) for x in (1, 0) if k < dist - 1 or x
+        ]
+
+    def places(k):
+        return dist - k, (nz - dist + k) % nz
+
+    have = set()
+
+    def ensure(h, j):
+        if (h, j) not in have:
+            if not any(half == h for half, _ in have):
+                prepare_weights(h)
+            compute_part(h, j)
+            have.add((h, j))
+
+    def ring_turn(i):
+        gather, h, long, k = turns[i]
         for d in range(2):
-            ag_arrived(h, d, dist - 1, d)
-        yield
-
-    def spread(g, step, count, start_one, sized):
-        def body(o, carry):
-            start_one(o).start()
-            return carry
-
-        lax.fori_loop(1, count, body, 0)
-
-        def wait_all():
-            probe = remote(sized, sized, g_send.at[g, step], g_recv.at[g, step], me, up)
-            probe.wait_recv()
-            probe.wait_send()
-
-        return wait_all
-
-    def gram_sum(g, src, ga, gb, full):
-        piece = src.shape[0] // nq
+            u = d if long else 1 - d
+            if gather:
+                if k > 0:
+                    ag_arrived(h, d, k - 1, u)
+                copy = ag_copy(h, d, k, u)
+                copy.start()
+                sent.append(copy)
+                continue
+            j = places(k)[d]
+            ensure(h, j)
+            if i == 0 and d == 0:
+                pl.semaphore_wait(barrier, seq_count - 1 + nz - 1)
+            if k == (0 if long else 1):
+                rs_send_unit(h, d, k, u, part.at[h, j, unit_rows(u)])
+            else:
+                rs_wait(h, d, k - 1, u)
+                slot = (k - 1) * 2 + u
+                ring[h, d, slot] = ring[h, d, slot] + part[h, j, unit_rows(u), :]
+                rs_send_unit(h, d, k, u, ring.at[h, d, slot])
+        for ahead in turns[i + 1 : i + 3]:
+            if not ahead[0]:
+                for j in places(ahead[3]):
+                    ensure(ahead[1], j)
+
+    progress = []
+
+    def ring_to(count):
+        while len(progress) < count:
+            ring_turn(len(progress))
+            progress.append(1)
+
+    def gather_last(h, long):
+        for d in range(2):
+            if long:
+                ag_arrived(h, d, dist - 1, d)
+            else:
+                ag_arrived(h, d, dist - 2, 1 - d)
+
+    def probe_of(sized, step):
+        return remote(sized, sized, g_send.at[step], g_recv.at[step], me, up)
+
+    def gram_sum():
+        piece = gsrc.shape[0] // seq_count
 
         def rows_of(i):
             return pl.ds(pl.multiple_of(i * piece, piece), piece)
 
-        def first(o):
-            peer, seq_id = xy_peer(o)
-            return remote(
-                src.at[rows_of(peer)], ga.at[q], g_send.at[g, 0], g_recv.at[g, 0], seq_id, z
-            )
-
-        wait_first = spread(g, 0, nq, first, ga.at[pl.ds(0, nq - 1)])
-        ga[q] = src[rows_of(q), :]
+        def first(o, carry):
+            peer = seq_peer(o)
+            remote(
+                gsrc.at[rows_of(peer)], ga.at[me], g_send.at[0], g_recv.at[0], peer, z
+            ).start()
+            return carry
+
+        lax.fori_loop(1, seq_count, first, 0)
+        ga[me] = gsrc[rows_of(me), :]
         yield
-        wait_first()
+        probe = probe_of(ga.at[pl.ds(0, seq_count - 1)], 0)
+        probe.wait_recv()
         value = ga[0]
-        for i in range(1, nq):
+        for i in range(1, seq_count):
             value = value + ga[i]
-        gb[mine] = value
-
-        def second(o):
-            seq_id, z_id = zc_peer(o)
-            return remote(gb.at[mine], gb.at[mine], g_send.at[g, 1], g_recv.at[g, 1], seq_id, z_id)
-
-        wait_second = spread(g, 1, members, second, gb.at[pl.ds(0, members - 1)])
+        gb[z] = value
+
+        def second(o, carry):
+            remote(
+                gb.at[z], gb.at[z], g_send.at[1], g_recv.at[1], me, lax.rem(z + o, nz)
+            ).start()
+            return carry
+
+        lax.fori_loop(1, nz, second, 0)
+        probe.wait_send()
         yield
-        wait_second()
+        probe = probe_of(gb.at[pl.ds(0, nz - 1)], 1)
+        probe.wait_recv()
         value = gb[0]
-        for i in range(1, members):
+        for i in range(1, nz):
             value = value + gb[i]
-        full[rows_of(q), :] = value
-
-        def third(o):
-            _, seq_id = xy_peer(o)
-            return remote(
-                full.at[rows_of(q)], full.at[rows_of(q)], g_send.at[g, 2], g_recv.at[g, 2],
-                seq_id, z,
-            )
-
-        wait_third = spread(g, 2, nq, third, full.at[pl.ds(0, (nq - 1) * piece)])
+        gfull[rows_of(me), :] = value
+
+        def third(o, carry):
+            remote(
+                gfull.at[rows_of(me)], gfull.at[rows_of(me)], g_send.at[2], g_recv.at[2],
+                seq_peer(o), z,
+            ).start()
+            return carry
+
+        lax.fori_loop(1, seq_count, third, 0)
+        probe.wait_send()
         yield
-        wait_third()
+        probe = probe_of(gfull.at[pl.ds(0, (seq_count - 1) * piece)], 2)
+        probe.wait_recv()
+        probe.wait_send()
         yield
 
     tile = min(512, feats)
@@ -402,89 +422,93 @@
             count += 1
         return None
 
-    rs = [reduce_scatter(h) for h in range(2)]
-    ag = [all_gather(h) for h in range(2)]
     coef = [coef_sum(h) for h in range(2)]
-    rs_steps = 1 + 2 * (dist - 1)
-
-    run(rs[0], rs_steps + 1)
-    run(rs[1], 2)
-    run(rs[0], 1)
     own = pl.ds(pl.multiple_of(z * chunk, chunk), chunk)
+    def pair(h, k):
+        product(h, nz - k, False)
+        product(h, k, False)
+
+    full = dist == 4
+    ring_to(12 if full else len(turns) // 2)
+    ensure(0, 0)
+    own_chunk(0)
+    ring_to(15 if full else 0)
     own0 = s_all[0, own, :]
-    gsrc0[...] = tn(own0, own0)
-    gram0 = gram_sum(0, gsrc0, ga0, gb0, gfull0)
-    run(gram0, 1)
-    run(rs[1], 1)
-    run(gram0, 1)
-    run(rs[1], rs_steps - 3)
-    run(ag[0], 1)
-    run(gram0, 1)
-    run(rs[1], 1)
-    run(rs[1], 1)
+    gsrc[:HALF] = tn(own0, own0)
+    gsrc[3 * HALF :] = jnp.zeros((HALF, HALF), F32)
+    ensure(1, 0)
+    ring_to(17 if full else 0)
+    own_chunk(1)
+    ring_to(18 if full else 0)
     own1 = s_all[1, own, :]
-    gsrc1[:HALF] = tn(own1, s_all[0, own, :])
-    gsrc1[HALF:] = tn(own1, own1)
-    gram1 = gram_sum(1, gsrc1, ga1, gb1, gfull1)
-    run(gram1, 1)
-    run(gram0, 1)
-    chol0 = inverse_factor(gfull0[...])
+    gsrc[HALF : 2 * HALF] = tn(own1, s_all[0, own, :])
+    gsrc[2 * HALF : 3 * HALF] = tn(own1, own1)
+    gram = gram_sum()
+    run(gram, 1)
+    ring_to(19 if full else 0)
+    product(0, 0, True)
+    product(1, 0, True)
+    if full:
+        ring_to(20)
+        pair(0, 1)
+        ring_to(23)
+        run(gram, 1)
+        pair(0, 2)
+        ring_to(24)
+        gather_last(0, 0)
+        pair(0, 3)
+        ring_to(25)
+        gather_last(0, 1)
+        product(0, 4, False, start_core(0))
+        ring_to(26)
+        run(gram, 1)
+        run(coef[0], 1)
+        pair(1, 1)
+        ring_to(27)
+        pair(1, 2)
+        ring_to(28)
+        gather_last(1, 0)
+        pair(1, 3)
+        gather_last(1, 1)
+        product(1, 4, False, start_core(1))
+    else:
+        ring_to(len(turns))
+        run(gram, 2)
+        for h in range(2):
+            gather_last(h, 0)
+            gather_last(h, 1)
+            for j in order[:-1]:
+                product(h, j, False, start_core(h) if j == order[-2] else None)
+        run(coef[0], 1)
+    run(gram, 1)
+    chol0 = inverse_factor(gfull[:HALF])
     run(chol0, 3)
-    run(gram1, 1)
-    run(ag[0], 1)
-    run(chol0, 4)
-    run(gram1, 1)
-    run(chol0, 3)
-    run(ag[0], 1)
+    run(coef[1], 1)
     w00 = run(chol0)
-    run(gram1)
-    low10 = nt(gfull1[:HALF], w00)
-    run(ag[0], dist - 3 if dist > 3 else 0)
-    run(ag[1], 1)
-    schur = gfull1[HALF:] - nt(low10, low10)
-    chol1 = inverse_factor(schur)
-    run(chol1, 4)
-    run(ag[0])
-    run(chol1, 2)
-    for i, j in enumerate(order):
-        product(0, j, i == 0, start_core(0) if i == nz - 1 else None)
-    run(ag[1], 1)
-    run(chol1, 4)
     run(coef[0], 1)
-    run(ag[1], 1)
+    low10 = nt(gfull[HALF : 2 * HALF], w00)
+    chol1 = inverse_factor(gfull[2 * HALF : 3 * HALF] - nt(low10, low10))
     mixed = nn(low10, w00)
     w11 = run(chol1)
-    run(ag[1], 1)
     w10 = -nn(w11, mixed)
-    run(coef[0], 1)
-    late = [dist]
-    if dist > 1:
-        late = [dist - 1, nz - dist + 1, dist]
-    early = [j for j in order if j not in late]
-    for i, j in enumerate(early):
-        product(1, j, i == 0)
-    run(ag[1])
+    root = math.sqrt(total)
+    step = min(256, rows)
+
+    def basis_half(h):
+        @pl.loop(0, rows // step)
+        def _(i):
+            at = pl.ds(pl.multiple_of(i * step, step), step)
+            if h == 0:
+                basis_out[at, :HALF] = nt(s_all[0, at, :], w00 * root)
+            else:
+                basis_out[at, HALF:] = nt(s_all[0, at, :], w10 * root) + nt(
+                    s_all[1, at, :], w11 * root
+                )
+
+    basis_half(0)
     run(coef[0])
-    for i, j in enumerate(late):
-        last = i == len(late) - 1
-        product(1, j, not early and i == 0, start_core(1) if last else None)
-    run(coef[1], 1)
-
-    root = math.sqrt(total)
-    b00, b10, b11 = w00 * root, w10 * root, w11 * root
-    basis_copies = []
-    step = min(256, rows)
-    for i in range(rows // step):
-        at = pl.ds(i * step, step)
-        left0, left1 = s_all[0, at, :], s_all[1, at, :]
-        basis_v[at, :HALF] = nt(left0, b00)
-        basis_v[at, HALF:] = nt(left0, b10) + nt(left1, b11)
-        copy = pltpu.make_async_copy(basis_v.at[at], basis_out.at[at], out_sem.at[i])
-        copy.start()
-        basis_copies.append(copy)
-
     run(coef[1])
-    block = 2 * HALF // (2 * nq)
+    block = 2 * HALF // seq_count
     outs[:HALF] = nn(w00, cg[0]) / root
     outs[HALF:] = (nn(w10, cg[0]) + nn(w11, cg[1])) / root
 
@@ -500,6 +524,8 @@
 
     lax.fori_loop(1, nq, last_hop, 0)
     landed[q] = outs[rows_for(me), :]
+
+    basis_half(1)
     sized = landed.at[pl.ds(0, nq - 1)]
     probe = remote(sized, sized, c_send.at[2, 0], c_recv.at[2, 0], me, up)
     probe.wait_recv()
@@ -509,8 +535,6 @@
 
     for copy in sent:
         copy.wait_send()
-    for copy in basis_copies:
-        copy.wait()
 
 
 def shards(mesh_shape, tokens, sketch):
@@ -531,7 +555,7 @@
             jax.ShapeDtypeStruct((k // seq, feats), F32),
         ),
         in_specs=[pl.BlockSpec(memory_space=pl.ANY)] * 2,
-        out_specs=(pl.BlockSpec(memory_space=pl.ANY), pl.BlockSpec(memory_space=pltpu.VMEM)),
+        out_specs=(pl.BlockSpec(memory_space=pltpu.VMEM),) * 2,
         scratch_shapes=[
             pltpu.VMEM((rows, feats), BF16),
             pltpu.VMEM((2, feats, HALF), F32),
@@ -539,14 +563,10 @@
             pltpu.VMEM((2, nz, chunk, HALF), F32),
             pltpu.VMEM((2, 2, nz, unit, HALF), F32),
             pltpu.VMEM((2, rows, HALF), F32),
-            pltpu.VMEM((HALF, HALF), F32),
-            pltpu.VMEM((k, HALF), F32),
-            pltpu.VMEM((nq, HALF // nq, HALF), F32),
-            pltpu.VMEM((nq, k // nq, HALF), F32),
-            pltpu.VMEM((2 * nz, HALF // nq, HALF), F32),
-            pltpu.VMEM((2 * nz, k // nq, HALF), F32),
-            pltpu.VMEM((HALF, HALF), F32),
-            pltpu.VMEM((k, HALF), F32),
+            pltpu.VMEM((4 * HALF, HALF), F32),
+            pltpu.VMEM((seq, 4 * HALF // seq, HALF), F32),
+            pltpu.VMEM((nz, 4 * HALF // seq, HALF), F32),
+            pltpu.VMEM((4 * HALF, HALF), F32),
             pltpu.VMEM((2, nq, HALF, HALF), F32),
             pltpu.VMEM((2, nq, HALF // 2, HALF), F32),
             pltpu.VMEM((2, nq, HALF // 2, HALF), F32),
@@ -554,18 +574,16 @@
             pltpu.VMEM((2, HALF, HALF), F32),
             pltpu.VMEM((k, HALF), F32),
             pltpu.VMEM((nq, k // seq, HALF), F32),
-            pltpu.VMEM((rows, k), F32),
             dma((nz,)),
             dma((2,)),
             dma((2, 2, nz)),
             dma((2, 2, nz)),
             dma((2, 2, nz)),
             dma((2, 2, nz)),
-            dma((2, 3)),
-            dma((2, 3)),
+            dma((3,)),
+            dma((3,)),
             dma((3, tiles + 2)),
             dma((3, tiles + 2)),
-            dma((max(1, rows // 256),)),
         ],
         compiler_params=pltpu.CompilerParams(
             collective_id=0, has_side_effects=True, vmem_limit_bytes=50 * 1024 * 1024

time: 102 us -> 80.8 us (0.79)
  Pallas kernels: 99 us -> 78.1 us
    pallas_call x1, Pallas kernels: 99 us -> 78.1 us  [shards(): pl.pallas_call(functools.partial(kernel, nq, nz, total), out_shape=(jax.S...]
where the time goes in v2:
time: 80.8 us; the launch traced here: 80.7 us
  Pallas kernels  78.1 us (97%)
  local copies, waits for them, and re-layouts  1.95 us (2%)
    pallas_call x1, Pallas kernels, shards(): pl.pallas_call(functools.partial(kernel, nq, nz, total), out_shape=(jax.S...  78.1 us
    unnamed x2, local copies, waits for them, and re-layouts  1.95 us

profile of v2, /device:TPU:1, one launch (start us, length us, event | category | flops | bytes accessed | tf_op | source)
XLA Modules:
  0.0 80.7 jit_solution(9259980456665068236)
XLA Ops:
  0.6 78.1 %shard_map.41 = (f32[2048,256]{1,0:T(8,128)S(1)}, f32[8,2048]{1,0:T(8,128)S(1)}) custom-call(bf16[2048,2048]{1,0:T(8,128)(2,1)} %tok_hbm.1, f32[2048,256]{1,0:T(8,128)} %sk_hbm.1), custom_call_target="tpu_custom_call" | custom-call | tf_op jit(solution)/shard_map/pallas_call | solution.py:551
  78.7 1.3 %copy.6 = f32[2048,256]{1,0:T(8,128)} copy(f32[2048,256]{1,0:T(8,128)S(1)} %get-tuple-element.4) | data formatting | bytes 4194304
  80.0 0.6 copy.7

commit v3 on v2

--- a/solution.py
+++ b/solution.py
@@ -13,7 +13,8 @@
 F32 = jnp.float32
 BF16 = jnp.bfloat16
 HALF = 128
-PANEL = 8
+PANEL = 16
+SUBS = 1
 
 
 def dot32(a, b, dims):
@@ -59,7 +60,9 @@
             here = sub == j
             rows = [jnp.broadcast_to(item[j : j + 1], (PANEL, HALF)) for item in work]
             pivot = rows[0]
-            factor = jnp.where(here, -1.0, work[0]) * (1.0 / pivot)
+            inverse = 1.0 / work[0]
+            scale = jnp.broadcast_to(inverse[j : j + 1], (PANEL, HALF))
+            factor = jnp.where(here, -1.0, work[0]) * scale
             kept = jnp.where(here, rows[-1], kept)
             pivots = jnp.where(here, pivot, pivots)
             work = [
@@ -70,11 +73,18 @@
         if first + PANEL < size:
             solved = work[0]
             count = size - first - PANEL
-            below_lane = lax.broadcasted_iota(jnp.int32, (count, HALF), 1)
-            update = jnp.where((below_lane >= first) & (below_lane < first + PANEL), 0.0, below)
-            for j in range(PANEL):
-                update = update - below[:, first + j : first + j + 1] * solved[j : j + 1]
-            rest = update
+            pieces = []
+            for begin, end in ((0, PANEL), (PANEL, count)):
+                if begin >= end:
+                    continue
+                low = below[begin:end]
+                low_lane = lax.broadcasted_iota(jnp.int32, (end - begin, HALF), 1)
+                update = jnp.where((low_lane >= first) & (low_lane < first + PANEL), 0.0, low)
+                terms = [low[:, first + j : first + j + 1] * solved[j : j + 1] for j in range(PANEL)]
+                while len(terms) > 1:
+                    terms = [a + b for a, b in zip(terms[::2], terms[1::2])]
+                pieces.append(update - terms[0])
+            rest = jnp.concatenate(pieces, axis=0) if len(pieces) > 1 else pieces[0]
         yield None
     return jnp.concatenate(done, axis=0)
 
@@ -91,6 +101,7 @@
     rows, feats = tok.shape
     chunk = rows // nz
     unit = chunk // 2
+    piece_rows = unit // SUBS
     dist = nz // 2
     me = lax.axis_index("seq")
     z = lax.axis_index("tp")
@@ -169,53 +180,53 @@
         both = jnp.dot(tok[at, :], weights[h], preferred_element_type=F32)
         part[h, j] = both[:, :HALF] + both[:, HALF:]
 
-    def unit_rows(u):
-        return pl.ds(u * unit, unit)
+    def part_rows(u, b):
+        return pl.ds(u * unit + b * piece_rows, piece_rows)
 
     sent = []
 
-    def rs_copy(h, d, s, u, src):
+    def rs_copy(h, d, s, u, b, src):
         slot = s * 2 + u
         return remote(
-            src, ring.at[h, d, slot], rs_send.at[h, d, slot], rs_recv.at[h, d, slot],
+            src, ring.at[h, d, slot, b], rs_send.at[h, d, slot, b], rs_recv.at[h, d, slot, b],
             me, up if d == 0 else down,
         )
 
-    def rs_send_unit(h, d, s, u, src):
-        copy = rs_copy(h, d, s, u, src)
+    def rs_send_unit(h, d, s, u, b, src):
+        copy = rs_copy(h, d, s, u, b, src)
         copy.start()
         sent.append(copy)
 
-    def rs_wait(h, d, s, u):
-        rs_copy(h, d, s, u, ring.at[h, d, s * 2 + u]).wait_recv()
+    def rs_wait(h, d, s, u, b):
+        rs_copy(h, d, s, u, b, ring.at[h, d, s * 2 + u, b]).wait_recv()
 
     def own_chunk(h):
         at = pl.multiple_of(z * chunk, chunk)
+        slot = (dist - 1) * 2
         for u in range(2):
-            for d in range(2):
-                rs_wait(h, d, dist - 1, u)
-        for u in range(2):
-            slot = (dist - 1) * 2 + u
-            value = part[h, 0, unit_rows(u), :] + ring[h, 0, slot] + ring[h, 1, slot]
-            s_all[h, pl.ds(at + u * unit, unit), :] = value
-
-    def ag_copy(h, d, k, u):
-        c = lax.rem(z + nz - k, nz) if d == 0 else lax.rem(z + k, nz)
-        at = pl.ds(pl.multiple_of(c * chunk + u * unit, unit), unit)
+            for b in range(SUBS):
+                for d in range(2):
+                    rs_wait(h, d, dist - 1, u, b)
+                value = part[h, 0, part_rows(u, b), :]
+                value = value + ring[h, 0, slot + u, b] + ring[h, 1, slot + u, b]
+                s_all[h, pl.ds(at + u * unit + b * piece_rows, piece_rows), :] = value
+
+    def ag_unit(h, d, k, u, b, c):
+        start = c * chunk + u * unit + b * piece_rows
+        at = pl.ds(pl.multiple_of(start, piece_rows), piece_rows)
         slot = k * 2 + u
         return remote(
-            s_all.at[h, at], s_all.at[h, at], ag_send.at[h, d, slot], ag_recv.at[h, d, slot],
+            s_all.at[h, at], s_all.at[h, at], ag_send.at[h, d, slot, b], ag_recv.at[h, d, slot, b],
             me, up if d == 0 else down,
         )
 
-    def ag_arrived(h, d, k, u):
+    def ag_copy(h, d, k, u, b):
+        c = lax.rem(z + nz - k, nz) if d == 0 else lax.rem(z + k, nz)
+        return ag_unit(h, d, k, u, b, c)
+
+    def ag_arrived(h, d, k, u, b):
         c = lax.rem(z + nz - k - 1, nz) if d == 0 else lax.rem(z + k + 1, nz)
-        at = pl.ds(pl.multiple_of(c * chunk + u * unit, unit), unit)
-        slot = k * 2 + u
-        remote(
-            s_all.at[h, at], s_all.at[h, at], ag_send.at[h, d, slot], ag_recv.at[h, d, slot],
-            me, up if d == 0 else down,
-        ).wait_recv()
+        ag_unit(h, d, k, u, b, c).wait_recv()
 
     if dist == 4:
         turns = [
@@ -245,26 +256,29 @@
 
     def ring_turn(i):
         gather, h, long, k = turns[i]
-        for d in range(2):
-            u = d if long else 1 - d
-            if gather:
-                if k > 0:
-                    ag_arrived(h, d, k - 1, u)
-                copy = ag_copy(h, d, k, u)
-                copy.start()
-                sent.append(copy)
-                continue
-            j = places(k)[d]
-            ensure(h, j)
-            if i == 0 and d == 0:
+        if not gather:
+            for j in places(k):
+                ensure(h, j)
+            if i == 0:
                 pl.semaphore_wait(barrier, seq_count - 1 + nz - 1)
-            if k == (0 if long else 1):
-                rs_send_unit(h, d, k, u, part.at[h, j, unit_rows(u)])
-            else:
-                rs_wait(h, d, k - 1, u)
-                slot = (k - 1) * 2 + u
-                ring[h, d, slot] = ring[h, d, slot] + part[h, j, unit_rows(u), :]
-                rs_send_unit(h, d, k, u, ring.at[h, d, slot])
+        for b in range(SUBS):
+            for d in range(2):
+                u = d if long else 1 - d
+                if gather:
+                    if k > 0:
+                        ag_arrived(h, d, k - 1, u, b)
+                    copy = ag_copy(h, d, k, u, b)
+                    copy.start()
+                    sent.append(copy)
+                    continue
+                j = places(k)[d]
+                if k == (0 if long else 1):
+                    rs_send_unit(h, d, k, u, b, part.at[h, j, part_rows(u, b)])
+                else:
+                    rs_wait(h, d, k - 1, u, b)
+                    slot = (k - 1) * 2 + u
+                    ring[h, d, slot, b] = ring[h, d, slot, b] + part[h, j, part_rows(u, b), :]
+                    rs_send_unit(h, d, k, u, b, ring.at[h, d, slot, b])
         for ahead in turns[i + 1 : i + 3]:
             if not ahead[0]:
                 for j in places(ahead[3]):
@@ -278,11 +292,12 @@
             progress.append(1)
 
     def gather_last(h, long):
-        for d in range(2):
-            if long:
-                ag_arrived(h, d, dist - 1, d)
-            else:
-                ag_arrived(h, d, dist - 2, 1 - d)
+        for b in range(SUBS):
+            for d in range(2):
+                if long:
+                    ag_arrived(h, d, dist - 1, d, b)
+                else:
+                    ag_arrived(h, d, dist - 2, 1 - d, b)
 
     def probe_of(sized, step):
         return remote(sized, sized, g_send.at[step], g_recv.at[step], me, up)
@@ -385,14 +400,13 @@
                 p = t * per_tile + i
                 cp[h, p] = c0[h, p, keep, :] + cx[h, p]
 
-        def body(o, carry):
-            peer, seq_id = xy_peer(o)
-            remote(
-                cp.at[h, peer], cr.at[h, q], c_send.at[h, tiles], c_recv.at[h, tiles], seq_id, z
-            ).start()
-            return carry
-
-        lax.fori_loop(1, nq, body, 0)
+                @pl.when(p != q)
+                def _(p=p):
+                    remote(
+                        cp.at[h, p], cr.at[h, q], c_send.at[h, tiles], c_recv.at[h, tiles],
+                        p * 2 + core, z,
+                    ).start()
+
         cr[h, q] = cp[h, q]
         yield
         sized = cr.at[h, pl.ds(0, nq - 1)]
@@ -451,8 +465,9 @@
     if full:
         ring_to(20)
         pair(0, 1)
+        ring_to(22)
+        run(gram, 1)
         ring_to(23)
-        run(gram, 1)
         pair(0, 2)
         ring_to(24)
         gather_last(0, 0)
@@ -480,12 +495,12 @@
             for j in order[:-1]:
                 product(h, j, False, start_core(h) if j == order[-2] else None)
         run(coef[0], 1)
+    run(coef[1], 1)
     run(gram, 1)
     chol0 = inverse_factor(gfull[:HALF])
-    run(chol0, 3)
-    run(coef[1], 1)
+    run(chol0, 4)
+    run(coef[0], 1)
     w00 = run(chol0)
-    run(coef[0], 1)
     low10 = nt(gfull[HALF : 2 * HALF], w00)
     chol1 = inverse_factor(gfull[2 * HALF : 3 * HALF] - nt(low10, low10))
     mixed = nn(low10, w00)
@@ -494,47 +509,54 @@
     root = math.sqrt(total)
     step = min(256, rows)
 
-    def basis_half(h):
+    def make_basis():
+        upper = jnp.concatenate([w00, jnp.zeros((HALF, HALF), F32)], axis=1)
+        factor = jnp.concatenate([upper, jnp.concatenate([w10, w11], axis=1)], axis=0) * root
+
         @pl.loop(0, rows // step)
         def _(i):
             at = pl.ds(pl.multiple_of(i * step, step), step)
-            if h == 0:
-                basis_out[at, :HALF] = nt(s_all[0, at, :], w00 * root)
-            else:
-                basis_out[at, HALF:] = nt(s_all[0, at, :], w10 * root) + nt(
-                    s_all[1, at, :], w11 * root
-                )
-
-    basis_half(0)
-    run(coef[0])
-    run(coef[1])
+            left = jnp.concatenate([s_all[0, at, :], s_all[1, at, :]], axis=1)
+            basis_out[at, :] = nt(left, factor)
+
     block = 2 * HALF // seq_count
-    outs[:HALF] = nn(w00, cg[0]) / root
-    outs[HALF:] = (nn(w10, cg[0]) + nn(w11, cg[1])) / root
 
     def rows_for(seq_id):
         return pl.ds(pl.multiple_of(seq_id * block, block), block)
 
-    def last_hop(o, carry):
-        _, seq_id = xy_peer(o)
-        remote(
-            outs.at[rows_for(seq_id)], landed.at[q], c_send.at[2, 0], c_recv.at[2, 0], seq_id, z
-        ).start()
-        return carry
-
-    lax.fori_loop(1, nq, last_hop, 0)
+    def deliver(first, count):
+        def body(p, carry):
+            @pl.when(p != q)
+            def _():
+                seq_id = p * 2 + core
+                remote(
+                    outs.at[rows_for(seq_id)], landed.at[q], c_send.at[2, 0], c_recv.at[2, 0],
+                    seq_id, z,
+                ).start()
+
+            return carry
+
+        lax.fori_loop(first, first + count, body, 0)
+
+    run(coef[0])
+    reduced0 = cg[0]
+    outs[:HALF] = nn(w00, reduced0) / root
+    deliver(0, nq // 2)
+    early = nn(w10, reduced0)
+    run(coef[1])
+    outs[HALF:] = (early + nn(w11, cg[1])) / root
+    deliver(nq // 2, nq // 2)
     landed[q] = outs[rows_for(me), :]
-
-    basis_half(1)
+    for copy in sent:
+        copy.wait_send()
+
+    make_basis()
     sized = landed.at[pl.ds(0, nq - 1)]
     probe = remote(sized, sized, c_send.at[2, 0], c_recv.at[2, 0], me, up)
     probe.wait_recv()
     probe.wait_send()
     for i in range(nq):
         coef_out[:, i * HALF : (i + 1) * HALF] = landed[i]
-
-    for copy in sent:
-        copy.wait_send()
 
 
 def shards(mesh_shape, tokens, sketch):
@@ -561,7 +583,7 @@
             pltpu.VMEM((2, feats, HALF), F32),
             pltpu.VMEM((2, feats, k), BF16),
             pltpu.VMEM((2, nz, chunk, HALF), F32),
-            pltpu.VMEM((2, 2, nz, unit, HALF), F32),
+            pltpu.VMEM((2, 2, nz, SUBS, unit // SUBS, HALF), F32),
             pltpu.VMEM((2, rows, HALF), F32),
             pltpu.VMEM((4 * HALF, HALF), F32),
             pltpu.VMEM((seq, 4 * HALF // seq, HALF), F32),
@@ -576,10 +598,10 @@
             pltpu.VMEM((nq, k // seq, HALF), F32),
             dma((nz,)),
             dma((2,)),
-            dma((2, 2, nz)),
-            dma((2, 2, nz)),
-            dma((2, 2, nz)),
-            dma((2, 2, nz)),
+            dma((2, 2, nz, SUBS)),
+            dma((2, 2, nz, SUBS)),
+            dma((2, 2, nz, SUBS)),
+            dma((2, 2, nz, SUBS)),
             dma((3,)),
             dma((3,)),
             dma((3, tiles + 2)),

time: 80.8 us -> 77.9 us (0.964); the launches traced: 80.7 us -> 76.9 us
  Pallas kernels: 78.1 us -> 74.3 us
    pallas_call x1, Pallas kernels: 78.1 us -> 74.3 us  [shards(): pl.pallas_call(functools.partial(kernel, nq, nz, total), out_shape=(jax.S...]
where the time goes in v3:
time: 77.9 us; the launch traced here: 76.9 us
  Pallas kernels  74.3 us (95%)
  local copies, waits for them, and re-layouts  1.95 us (3%)
    pallas_call x1, Pallas kernels, shards(): pl.pallas_call(functools.partial(kernel, nq, nz, total), out_shape=(jax.S...  74.3 us
    unnamed x2, local copies, waits for them, and re-layouts  1.95 us

profile of v3, /device:TPU:1, one launch (start us, length us, event | category | flops | bytes accessed | tf_op | source)
XLA Modules:
  0.0 76.9 jit_solution(11856032534046031917)
XLA Ops:
  0.6 74.3 %shard_map.41 = (f32[2048,256]{1,0:T(8,128)S(1)}, f32[8,2048]{1,0:T(8,128)S(1)}) custom-call(bf16[2048,2048]{1,0:T(8,128)(2,1)} %tok_hbm.1, f32[2048,256]{1,0:T(8,128)} %sk_hbm.1), custom_call_target="tpu_custom_call" | custom-call | tf_op jit(solution)/shard_map/pallas_call | solution.py:573
  74.9 1.3 %copy.6 = f32[2048,256]{1,0:T(8,128)} copy(f32[2048,256]{1,0:T(8,128)S(1)} %get-tuple-element.4) | data formatting | bytes 4194304
  76.2 0.6 copy.7

commit v4 on v3

--- a/solution.py
+++ b/solution.py
@@ -140,9 +140,6 @@
         tok_copies[j] = pltpu.make_async_copy(tok_hbm.at[at], tok.at[at], tok_sem.at[j])
     sk_copies[0].start()
     tok_copies[order[0]].start()
-    sk_copies[1].start()
-    for j in order[1:]:
-        tok_copies[j].start()
 
     barrier = pltpu.get_barrier_semaphore()
 
@@ -159,7 +156,11 @@
     lax.fori_loop(1, nz, greet_z, 0)
     lax.fori_loop(1, seq_count, greet_seq, 0)
 
-    loaded = set()
+    tok_copies[order[0]].wait()
+    loaded = {order[0]}
+    sk_copies[1].start()
+    for j in order[1:]:
+        tok_copies[j].start()
 
     def prepare_weights(h):
         sk_copies[h].wait()
@@ -498,9 +499,8 @@
     run(coef[1], 1)
     run(gram, 1)
     chol0 = inverse_factor(gfull[:HALF])
-    run(chol0, 4)
+    w00 = run(chol0)
     run(coef[0], 1)
-    w00 = run(chol0)
     low10 = nt(gfull[HALF : 2 * HALF], w00)
     chol1 = inverse_factor(gfull[2 * HALF : 3 * HALF] - nt(low10, low10))
     mixed = nn(low10, w00)

time: 77.9 us -> 77.9 us (level)
  no operation moved by 1% of the time
where the time goes in v4:
time: 77.9 us; the launch traced here: 77 us
  Pallas kernels  74.4 us (96%)
  local copies, waits for them, and re-layouts  1.95 us (3%)
    pallas_call x1, Pallas kernels, shards(): pl.pallas_call(functools.partial(kernel, nq, nz, total), out_shape=(jax.S...  74.4 us
    unnamed x2, local copies, waits for them, and re-layouts  1.95 us

profile of v4, /device:TPU:1, one launch (start us, length us, event | category | flops | bytes accessed | tf_op | source)
XLA Modules:
  0.0 77.0 jit_solution(7523049885370096134)
XLA Ops:
  0.6 74.4 %shard_map.41 = (f32[2048,256]{1,0:T(8,128)S(1)}, f32[8,2048]{1,0:T(8,128)S(1)}) custom-call(bf16[2048,2048]{1,0:T(8,128)(2,1)} %tok_hbm.1, f32[2048,256]{1,0:T(8,128)} %sk_hbm.1), custom_call_target="tpu_custom_call" | custom-call | tf_op jit(solution)/shard_map/pallas_call | solution.py:573
  75.1 1.3 %copy.6 = f32[2048,256]{1,0:T(8,128)} copy(f32[2048,256]{1,0:T(8,128)S(1)} %get-tuple-element.4) | data formatting | bytes 4194304
  76.4 0.6 copy.7
